TPU v7x, 256 devices: a whole 4x4x8 slice. The times are simulated.
256 devices in a mesh: dp: 4 (over y), gx: 4 (over x), gy: 16 (over z, core).
Axes of the slice: x: 4, y: 4, z: 8, core: 2. Of those that a mesh axis runs over, the one named last changes fastest.
Arguments:
- field: bfloat16 [4, 64, 32, 20, 2048], P('dp', 'gx', 'gy'), may hold values from -6 to 6
- cotangent: bfloat16 [4, 64, 32, 20, 2048], P('dp', 'gx', 'gy'), may hold values from -6 to 6
- spectral_weight: bfloat16 [24, 24, 20, 20, 192], P(None, None, None, None, ('gx', 'gy')), may hold values from -2.5 to 2.5
- bypass_weight: bfloat16 [20, 20], replicated, may hold values from -1.25 to 1.25
Outputs:
- grad_field: bfloat16 [4, 64, 32, 20, 2048], P('dp', 'gx', 'gy')
- grad_spectral: float32 [24, 24, 20, 20, 192], P(None, None, None, None, ('gx', 'gy'))
- grad_bypass: float32 [20, 20], replicated
All inputs are finite; a program needn't handle non-finite values.
Results may differ from a plain program's by a relative error of at most 0.034.
Values may be sent and summed in bfloat16 or wider, within the bound.
No kernel may reach another device: no remote copies, remote signals or barrier semaphores. Data moves between devices by JAX's collectives and lax.ppermute only.
A program may use at most 192 MiB of HBM per device.

v0:
```python
import math
import jax
import jax.numpy as jnp
from jax import lax
from jax.sharding import PartitionSpec as P

MX = 12
MY = 12
MZ = 12
MT = 4
NZ = 128
NT = 16


def basis(length, kept):
    places = lax.iota(jnp.int32, length)
    orders = lax.iota(jnp.int32, kept)
    cos_arg = places[:, None] * orders[None, :] % length
    sin_arg = places[:, None] * (orders[None, :] + 1) % length
    step_angle = 2.0 * math.pi / length
    scale = math.sqrt(2.0 / length)
    cos_part = jnp.cos(cos_arg.astype(jnp.float32) * step_angle)
    sin_part = jnp.sin(sin_arg.astype(jnp.float32) * step_angle)
    return jnp.concatenate([cos_part, sin_part], axis=1) * scale


def mode_dot(form, data, table):
    upper = table.astype(jnp.bfloat16)
    lower = (table - upper.astype(jnp.float32)).astype(jnp.bfloat16)
    first = jnp.einsum(form, data, upper, preferred_element_type=jnp.float32)
    return first + jnp.einsum(form, data, lower, preferred_element_type=jnp.float32)


def body(field, cotangent, spectral_weight, bypass_weight):
    cells_x = field.shape[1]
    cells_y = field.shape[2]
    channels = field.shape[3]
    parts_x = lax.axis_size("gx")
    parts_y = lax.axis_size("gy")
    table_x = basis(cells_x * parts_x, MX)
    table_y = basis(cells_y * parts_y, MY)
    table_z = basis(NZ, MZ)
    table_t = basis(NT, MT)
    modes_zt = 4 * MZ * MT
    table_zt = (table_z[:, None, :, None] * table_t[None, :, None, :]).reshape(NZ * NT, modes_zt)

    def analyze(cells):
        matrix = cells.reshape(-1, NZ * NT)
        coeff = mode_dot("rp,pq->rq", matrix, table_zt).astype(jnp.bfloat16)
        coeff = coeff.reshape(cells_x, cells_y, channels, modes_zt)
        along_x = lax.all_to_all(coeff, "gx", split_axis=3, concat_axis=0, tiled=True)
        partial_x = mode_dot("xycq,xk->kycq", along_x, table_x).astype(jnp.bfloat16)
        along_y = lax.all_to_all(partial_x, "gy", split_axis=3, concat_axis=1, tiled=True)
        return mode_dot("kycq,yl->klcq", along_y, table_y).astype(jnp.bfloat16)

    def synthesize(spectrum):
        partial_y = mode_dot("klcq,yl->kycq", spectrum, table_y).astype(jnp.bfloat16)
        returned = lax.all_to_all(partial_y, "gy", split_axis=1, concat_axis=3, tiled=True)
        partial_x = mode_dot("kycq,xk->xycq", returned, table_x).astype(jnp.bfloat16)
        coeff = lax.all_to_all(partial_x, "gx", split_axis=0, concat_axis=3, tiled=True)
        matrix = coeff.reshape(-1, modes_zt)
        values = mode_dot("rq,pq->rp", matrix, table_zt)
        return values.reshape(1, cells_x, cells_y, channels, NZ * NT)

    spectrum = analyze(field)
    mixed = jnp.einsum(
        "klcq,klcoq->kloq", spectrum, spectral_weight, preferred_element_type=jnp.float32
    ).astype(jnp.bfloat16)
    spatial = synthesize(mixed)
    bypass = jnp.einsum("bxyip,io->bxyop", field, bypass_weight, preferred_element_type=jnp.float32)
    pre = spatial + bypass
    unused, pullback = jax.vjp(jax.nn.gelu, pre)
    (slope,) = pullback(cotangent.astype(jnp.float32))
    upstream = slope.astype(jnp.bfloat16)
    bypass_term = jnp.einsum("bxyip,bxyop->io", field, upstream, preferred_element_type=jnp.float32)
    grad_bypass = lax.psum(bypass_term, ("dp", "gx", "gy"))
    spectrum_up = analyze(upstream)
    local_grad = jnp.einsum(
        "klcq,kloq->klcoq", spectrum, spectrum_up, preferred_element_type=jnp.float32
    )
    grad_spectral = lax.psum(local_grad.astype(jnp.bfloat16), "dp").astype(jnp.float32)
    spectrum_back = jnp.einsum(
        "kloq,klcoq->klcq", spectrum_up, spectral_weight, preferred_element_type=jnp.float32
    ).astype(jnp.bfloat16)
    through_bypass = jnp.einsum(
        "bxyop,io->bxyip", upstream, bypass_weight, preferred_element_type=jnp.float32
    )
    grad_field = (synthesize(spectrum_back) + through_bypass).astype(jnp.bfloat16)
    return (grad_field, grad_spectral, grad_bypass)


def solution(mesh):
    in_specs = (
        P("dp", "gx", "gy", None, None),
        P("dp", "gx", "gy", None, None),
        P(None, None, None, None, ("gx", "gy")),
        P(),
    )
    out_specs = (P("dp", "gx", "gy", None, None), P(None, None, None, None, ("gx", "gy")), P())
    return jax.shard_map(body, mesh=mesh, in_specs=in_specs, out_specs=out_specs, check_vma=False)
```

profile of v0, /device:TPU:1, one launch (start us, length us, event | category | flops | bytes accessed | tf_op | source)
XLA Modules:
  0.0 493.5 jit_solution(16601009664940160456)
XLA Ops:
  7.5 4.7 copy.145
  15.8 6.2 %fusion = (bf16[128,16,24,8]{1,0,3,2:T(8,128)(2,1)}, bf16[128,16,24,8]{1,0,3,2:T(8,128)(2,1)}) fusion(f32[16,8]{0,1:T(8,128)S(1)} %maximum_multiply_fusion.3, f32[128,24]{0,1:T(8,128)S(1)} %maximum_multiply_fusion.2), kind=kLoop, calls=%fused_computation.5 | loop fusion | flops 1966080 | bytes 1585664 | tf_op jit(solution)/shard_map/convert_element_type | solution.py:29
  22.0 11.6 %convert_element_type.256 = bf16[2048,192]{0,1:T(8,128)(2,1)S(1)} reshape(bf16[128,16,24,8]{1,0,3,2:T(8,128)(2,1)} %get-tuple-element.26) | data formatting | bytes 1572864 | tf_op jit(solution)/shard_map/convert_element_type | solution.py:29
  33.7 12.3 %convert_element_type.253 = bf16[2048,192]{0,1:T(8,128)(2,1)} reshape(bf16[128,16,24,8]{1,0,3,2:T(8,128)(2,1)} %get-tuple-element.27) | data formatting | bytes 1572864 | tf_op jit(solution)/shard_map/convert_element_type | solution.py:28
  49.9 5.9 %reshape.160 = bf16[16,2,20,192]{2,1,0,3:T(2,128)(2,1)S(1)} reshape(bf16[640,192]{0,1:T(8,128)(2,1)} %fusion.30) | data formatting | bytes 491520 | tf_op jit(solution)/shard_map/reshape | solution.py:50
  55.9 4.2 reshape.162
  60.0 4.8 all-to-all-start
  65.0 5.3 %all-to-all-done = bf16[4,2,15360]{2,1,0:T(2,128)(2,1)S(1)} async-done(((bf16[4,2,15360]{2,1,0:T(2,128)(2,1)}), bf16[4,2,15360]{2,1,0:T(2,128)(2,1)S(1)}, u32[]{:S(2)}, u32[]{:S(2)}) %all-to-all-start) | async-done | bytes 245792 | tf_op jit(solution)/shard_map/all_to_all | solution.py:51
  70.3 4.1 reshape.163
  79.3 10.9 %all-to-all-start.1 = ((bf16[16,2,1440]{2,1,0:T(2,128)(2,1)}), bf16[16,2,1440]{2,1,0:T(2,128)(2,1)S(1)}, u32[]{:S(2)}, u32[]{:S(2)}) async-start(bf16[16,2,1440]{2,1,0:T(2,128)(2,1)} %reshape.164), calls=%async_computation.1 | async-start | bytes 196608 | tf_op jit(solution)/shard_map/all_to_all | solution.py:53
  90.4 8.2 %all-to-all-done.1 = bf16[16,2,1440]{2,1,0:T(2,128)(2,1)S(1)} async-done(((bf16[16,2,1440]{2,1,0:T(2,128)(2,1)}), bf16[16,2,1440]{2,1,0:T(2,128)(2,1)S(1)}, u32[]{:S(2)}, u32[]{:S(2)}) %all-to-all-start.1) | async-done | bytes 92192 | tf_op jit(solution)/shard_map/all_to_all | solution.py:53
  101.2 5.0 %multiply_reduce_fusion.1 = bf16[24,24,3,20]{1,0,2,3:T(8,128)(2,1)S(1)} fusion(f32[24,24,3,20]{1,0,2,3:T(8,128)S(1)} %copy.223, bf16[24,24,20,20,3]{1,0,4,3,2:T(8,128)(2,1)} %param.6), kind=kLoop, calls=%fused_computation.3 | loop fusion | flops 2039040 | bytes 1589760 | tf_op jit(solution)/shard_map/klcq,klcoq->kloq/dot_general | solution.py:66
  107.7 10.9 %all_to_all.138 = bf16[16,2,1440]{2,1,0:T(2,128)(2,1)S(1)} all-to-all(bf16[16,2,1440]{2,1,0:T(2,128)(2,1)S(1)} %reshape.166), channel_id=1, replica_groups=mesh['dp'=4,'gx'=4,'gy'=16] {'gy'}, dimensions={0} | all-to-all | bytes 184320 | tf_op jit(solution)/shard_map/all_to_all | solution.py:58
  122.3 9.6 %all_to_all.139 = bf16[4,2,15360]{2,1,0:T(2,128)(2,1)S(1)} all-to-all(bf16[4,2,15360]{2,1,0:T(2,128)(2,1)S(1)} %reshape.168), channel_id=1, replica_groups=mesh['dp'=4,'gx'=4,'gy'=16] {'gx'}, dimensions={0} | all-to-all | bytes 491520 | tf_op jit(solution)/shard_map/all_to_all | solution.py:60
  139.5 6.7 %reshape.142 = f32[1,16,2,20,2048]{4,3,2,1,0:T(8,128)} reshape(f32[640,2048]{1,0:T(8,128)} %convolution_add_fusion.1) | data formatting | bytes 10485760 | tf_op jit(solution)/shard_map/reshape | solution.py:63
  146.1 11.0 %fusion.4 = bf16[1,16,2,20,2048]{4,3,2,1,0:T(8,128)(2,1)} fusion(f32[1,16,2,20,2048]{4,3,2,1,0:T(8,128)} %reshape.142, bf16[1,16,2,20,2048]{4,2,3,1,0:T(2,128)(2,1)} %param.5, bf16[16,2,20,2048]{3,1,2,0:T(2,128)(2,1)} %bitcast.208, bf16[20,20]{1,0:T(8,128)(2,1)S(1)} %copy-done), kind=kOutput, calls=%fused_computation.13 | convolution fusion | flops 81264640 | bytes 13108000 | tf_op jit(solution)/shard_map/bxyip,io->bxyop/dot_general | solution.py:70
  157.1 5.3 %reshape.144 = bf16[640,2048]{1,0:T(8,128)(2,1)} reshape(bf16[1,16,2,20,2048]{4,3,2,1,0:T(8,128)(2,1)} %fusion.4) | data formatting | bytes 5242880 | tf_op jit(solution)/shard_map/reshape | solution.py:48
  168.0 3.8 reshape.161
  175.3 8.8 %all_to_all.140 = bf16[4,2,15360]{2,1,0:T(2,128)(2,1)} all-to-all(bf16[4,2,15360]{2,1,0:T(2,128)(2,1)S(1)} %reshape.170), channel_id=1, replica_groups=mesh['dp'=4,'gx'=4,'gy'=16] {'gx'}, dimensions={0} | all-to-all | bytes 491520 | tf_op jit(solution)/shard_map/all_to_all | solution.py:51
  184.2 6.0 %reshape.171 = bf16[192,16,2,20]{3,2,1,0:T(2,128)(2,1)S(1)} reshape(bf16[4,2,15360]{2,1,0:T(2,128)(2,1)} %all_to_all.140) | data formatting | bytes 491520
  196.9 5.2 %all-to-all-start.5 = ((bf16[16,2,1440]{2,1,0:T(2,128)(2,1)}), bf16[16,2,1440]{2,1,0:T(2,128)(2,1)S(1)}, u32[]{:S(2)}, u32[]{:S(2)}) async-start(bf16[16,2,1440]{2,1,0:T(2,128)(2,1)} %reshape.172), calls=%async_computation.5 | async-start | bytes 196608 | tf_op jit(solution)/shard_map/all_to_all | solution.py:53
  204.3 6.3 %all-to-all-done.5 = bf16[16,2,1440]{2,1,0:T(2,128)(2,1)S(1)} async-done(((bf16[16,2,1440]{2,1,0:T(2,128)(2,1)}), bf16[16,2,1440]{2,1,0:T(2,128)(2,1)S(1)}, u32[]{:S(2)}, u32[]{:S(2)}) %all-to-all-start.5) | async-done | bytes 92192 | tf_op jit(solution)/shard_map/all_to_all | solution.py:53
  214.5 5.0 %multiply_reduce_fusion = bf16[24,24,3,20]{1,0,2,3:T(8,128)(2,1)S(1)} fusion(f32[24,24,3,20]{1,0,2,3:T(8,128)S(1)} %copy.224, bf16[24,24,20,20,3]{1,0,4,3,2:T(8,128)(2,1)} %param.6), kind=kLoop, calls=%fused_computation.2 | loop fusion | flops 2039040 | bytes 1589760 | tf_op jit(solution)/shard_map/kloq,klcoq->klcq/dot_general | solution.py:82
  221.6 3.7 all-to-all-start.6
  225.3 4.9 fusion.31
  230.2 76.2 %psum.15 = f32[20,20]{0,1:T(8,128)S(1)} all-reduce(f32[20,20]{0,1:T(8,128)S(1)} %fusion.31), channel_id=1, replica_groups=mesh['dp'=4,'gx'=4,'gy'=16] {'dp','gx','gy'}, use_global_device_ids=true, to_apply=%region_1.2 | all-reduce | flops 400 | bytes 3200 | tf_op jit(solution)/shard_map/psum | solution.py:76
  321.4 5.3 %fusion.1 = bf16[24,24,20,20,3]{1,0,4,3,2:T(8,128)(2,1)} fusion(f32[24,24,3,20]{1,0,2,3:T(8,128)S(1)} %copy-done.3, f32[24,24,3,20]{1,0,2,3:T(8,128)} %copy.186), kind=kLoop, calls=%fused_computation.10 | loop fusion | flops 1382400 | bytes 1658880 | tf_op jit(solution)/shard_map/convert_element_type | solution.py:81
  334.4 7.2 %reshape.147 = f32[1,16,2,20,2048]{4,3,2,1,0:T(8,128)} reshape(f32[640,2048]{1,0:T(8,128)} %convolution_add_fusion) | data formatting | bytes 10485760 | tf_op jit(solution)/shard_map/reshape | solution.py:63
  341.6 4.1 fusion.12
  345.7 4.2 copy.189
  349.9 126.0 %all-reduce.2.cloned.1.call-done = bf16[24,24,20,20,3]{1,0,4,3,2:T(8,128)(2,1)} async-done(((bf16[24,24,20,20,3]{1,0,4,3,2:T(8,128)(2,1)}), bf16[24,24,20,20,3]{1,0,4,3,2:T(8,128)(2,1)}) %all-reduce.2.cloned.1.call-update) | async-done | bytes 1382416 | tf_op jit(solution)/shard_map/psum | solution.py:81
  475.9 10.2 %convert_element_type.284 = f32[24,24,20,20,3]{1,0,4,3,2:T(8,128)} convert(bf16[24,24,20,20,3]{1,0,4,3,2:T(8,128)(2,1)} %all-reduce.2.cloned.1.call-done) | non-fusion elementwise | flops 691200 | bytes 4147200 | tf_op jit(solution)/shard_map/convert_element_type | solution.py:81
  (90 shorter events, 74.8 us)
Async XLA Ops:
  7.2 139.0 %copy-start = (bf16[20,20]{1,0:T(8,128)(2,1)S(1)}, bf16[20,20]{1,0:T(8,128)(2,1)}, u32[]{:S(2)}) copy-start(bf16[20,20]{1,0:T(8,128)(2,1)} %param.7) | copy-start | bytes 2404
  60.0 10.3 %all-to-all-start = ((bf16[4,2,15360]{2,1,0:T(2,128)(2,1)}), bf16[4,2,15360]{2,1,0:T(2,128)(2,1)S(1)}, u32[]{:S(2)}, u32[]{:S(2)}) async-start(bf16[4,2,15360]{2,1,0:T(2,128)(2,1)} %reshape.162), calls=%async_computation | async-start | bytes 491520 | tf_op jit(solution)/shard_map/all_to_all | solution.py:51
  79.3 19.3 %all-to-all-start.1 = ((bf16[16,2,1440]{2,1,0:T(2,128)(2,1)}), bf16[16,2,1440]{2,1,0:T(2,128)(2,1)S(1)}, u32[]{:S(2)}, u32[]{:S(2)}) async-start(bf16[16,2,1440]{2,1,0:T(2,128)(2,1)} %reshape.164), calls=%async_computation.1 | async-start | bytes 196608 | tf_op jit(solution)/shard_map/all_to_all | solution.py:53
  119.1 16.2 %copy-start.1 = (bf16[2048,192]{0,1:T(8,128)(2,1)S(1)}, bf16[2048,192]{0,1:T(8,128)(2,1)}, u32[]{:S(2)}) copy-start(bf16[2048,192]{0,1:T(8,128)(2,1)} %convert_element_type.253) | copy-start | bytes 2359300
  196.9 13.7 %all-to-all-start.5 = ((bf16[16,2,1440]{2,1,0:T(2,128)(2,1)}), bf16[16,2,1440]{2,1,0:T(2,128)(2,1)S(1)}, u32[]{:S(2)}, u32[]{:S(2)}) async-start(bf16[16,2,1440]{2,1,0:T(2,128)(2,1)} %reshape.172), calls=%async_computation.5 | async-start | bytes 196608 | tf_op jit(solution)/shard_map/all_to_all | solution.py:53
  221.6 87.7 %all-to-all-start.6 = ((bf16[16,2,1440]{2,1,0:T(2,128)(2,1)}), bf16[16,2,1440]{2,1,0:T(2,128)(2,1)S(1)}, u32[]{:S(2)}, u32[]{:S(2)}) async-start(bf16[16,2,1440]{2,1,0:T(2,128)(2,1)} %reshape.174), calls=%async_computation.6 | async-start | bytes 196608 | tf_op jit(solution)/shard_map/all_to_all | solution.py:58
  230.2 91.2 %copy-start.3 = (f32[24,24,3,20]{1,0,2,3:T(8,128)S(1)}, f32[24,24,3,20]{1,0,2,3:T(8,128)}, u32[]{:S(2)}) copy-start(f32[24,24,3,20]{1,0,2,3:T(8,128)} %copy.187) | copy-start | bytes 414724
  317.9 9.0 %all-to-all-start.7 = ((bf16[4,2,15360]{2,1,0:T(2,128)(2,1)}), bf16[4,2,15360]{2,1,0:T(2,128)(2,1)S(1)}, u32[]{:S(2)}, u32[]{:S(2)}) async-start(bf16[4,2,15360]{2,1,0:T(2,128)(2,1)} %reshape.176), calls=%async_computation.7 | async-start | bytes 491520 | tf_op jit(solution)/shard_map/all_to_all | solution.py:60
  321.3 154.6 %all-reduce.2.cloned.1.call-start = ((), (), s32[]{:S(2)}) async-start(), calls=%async_computation.8 | async-start | bytes 14745600 | tf_op jit(solution)/shard_map/psum | solution.py:81
  334.4 7.2 %copy-start.2 = (bf16[1,16,2,20,2048]{4,3,2,1,0:T(8,128)(2,1)S(1)}, bf16[1,16,2,20,2048]{4,3,2,1,0:T(8,128)(2,1)}, u32[]{:S(2)}) copy-start(bf16[1,16,2,20,2048]{4,3,2,1,0:T(8,128)(2,1)} %fusion.4) | copy-start | bytes 7864324
Sparse Core Ops, SparseCore 0:
  326.8 149.0 all-reduce.1
where the time goes:
time: 503 us; the launch traced here: 493 us
  waiting for transfers between devices  146 us (29%)
  local copies, waits for them, and re-layouts  120 us (24%)
  blocking collectives  105 us (21%)
  matrix products  46.5 us (9%)
  other arithmetic  32.3 us (6%)
  starting transfers between devices  28 us (6%)
  between operations  15.1 us (3%)
    psum x1, waiting for transfers between devices, body(): lax.psum(local_grad.astype(jnp.bfloat16), 'dp').astype(jnp.float32)  126 us
    psum x1, blocking collectives, body(): grad_bypass = lax.psum(bypass_term, ('dp', 'gx', 'gy'))  76.2 us
    unnamed x29, local copies, waits for them, and re-layouts  39.6 us
    dot_general x12, matrix products, mode_dot(): jnp.einsum(form, data, lower, preferred_element_type=jnp.float32)  16.9 us
    all_to_all x2, starting transfers between devices, analyze(): lax.all_to_all(partial_x, 'gy', split_axis=3, concat_axis=1, tiled=True)  16.1 us
    all_to_all x2, waiting for transfers between devices, analyze(): lax.all_to_all(partial_x, 'gy', split_axis=3, concat_axis=1, tiled=True)  14.5 us
    reshape x2, local copies, waits for them, and re-layouts, synthesize(): return values.reshape(1, cells_x, cells_y, channels, NZ * NT)  13.9 us
    convert_element_type x1, local copies, waits for them, and re-layouts, mode_dot(): upper = table.astype(jnp.bfloat16)  12.3 us
  transfers between devices with their start and end apart: 6, of which 5 were waited for; matrix products, arithmetic and copies ran while one was open for 8% of the time, Pallas kernels for 0%

commit v1 on v0

--- a/solution.py
+++ b/solution.py
@@ -73,7 +73,8 @@
     (slope,) = pullback(cotangent.astype(jnp.float32))
     upstream = slope.astype(jnp.bfloat16)
     bypass_term = jnp.einsum("bxyip,bxyop->io", field, upstream, preferred_element_type=jnp.float32)
-    grad_bypass = lax.psum(bypass_term, ("dp", "gx", "gy"))
+    half = lax.psum(bypass_term, ("gx", "gy"))
+    grad_bypass = lax.psum(half, "dp")
     spectrum_up = analyze(upstream)
     local_grad = jnp.einsum(
         "klcq,kloq->klcoq", spectrum, spectrum_up, preferred_element_type=jnp.float32

time: 503 us -> 688 us (1.37)
  blocking collectives: 105 us -> 287 us
    psum x1 -> x2, blocking collectives: 76.2 us -> 258 us  [the longest x1 244 us: body(): half = lax.psum(bypass_term, ('gx', 'gy'))]
  transfers between devices with their start and end apart: 6 -> 6, of which waited for: 5 -> 4; matrix products, arithmetic and copies ran while one was open for 8% -> 6% of each run, Pallas kernels for 0% -> 0%
where the time goes in v1:
time: 688 us; the launch traced here: 678 us
  blocking collectives  287 us (42%)
  waiting for transfers between devices  149 us (22%)
  local copies, waits for them, and re-layouts  120 us (17%)
  matrix products  46.9 us (7%)
  other arithmetic  32.3 us (5%)
  starting transfers between devices  28 us (4%)
  between operations  15.1 us (2%)
    psum x1, blocking collectives, body(): half = lax.psum(bypass_term, ('gx', 'gy'))  244 us
    psum x1, waiting for transfers between devices, body(): lax.psum(local_grad.astype(jnp.bfloat16), 'dp').astype(jnp.float32)  129 us
    unnamed x29, local copies, waits for them, and re-layouts  39.6 us
    dot_general x12, matrix products, mode_dot(): jnp.einsum(form, data, lower, preferred_element_type=jnp.float32)  16.8 us
    all_to_all x2, starting transfers between devices, analyze(): lax.all_to_all(partial_x, 'gy', split_axis=3, concat_axis=1, tiled=True)  16.1 us
    all_to_all x2, waiting for transfers between devices, analyze(): lax.all_to_all(partial_x, 'gy', split_axis=3, concat_axis=1, tiled=True)  14.5 us
    reshape x2, local copies, waits for them, and re-layouts, synthesize(): return values.reshape(1, cells_x, cells_y, channels, NZ * NT)  13.9 us
  transfers between devices with their start and end apart: 6, of which 4 were waited for; matrix products, arithmetic and copies ran while one was open for 6% of the time, Pallas kernels for 0%

profile of v1, /device:TPU:1, one launch (start us, length us, event | category | flops | bytes accessed | tf_op | source)
XLA Modules:
  0.0 678.5 jit_solution(7607641703787441757)
XLA Ops:
  7.5 4.7 copy.145
  15.8 6.2 fusion
  22.0 11.6 %convert_element_type.256 = bf16[2048,192]{0,1:T(8,128)(2,1)S(1)} reshape(bf16[128,16,24,8]{1,0,3,2:T(8,128)(2,1)} %get-tuple-element.26) | data formatting | bytes 1572864 | tf_op jit(solution)/shard_map/convert_element_type | solution.py:29
  33.7 12.3 %convert_element_type.253 = bf16[2048,192]{0,1:T(8,128)(2,1)} reshape(bf16[128,16,24,8]{1,0,3,2:T(8,128)(2,1)} %get-tuple-element.27) | data formatting | bytes 1572864 | tf_op jit(solution)/shard_map/convert_element_type | solution.py:28
  49.9 5.9 reshape.160
  55.9 4.2 reshape.162
  60.0 4.8 all-to-all-start
  65.0 5.3 all-to-all-done
  70.3 4.1 reshape.163
  79.3 10.9 %all-to-all-start.1 = ((bf16[16,2,1440]{2,1,0:T(2,128)(2,1)}), bf16[16,2,1440]{2,1,0:T(2,128)(2,1)S(1)}, u32[]{:S(2)}, u32[]{:S(2)}) async-start(bf16[16,2,1440]{2,1,0:T(2,128)(2,1)} %reshape.164), calls=%async_computation.1 | async-start | bytes 196608 | tf_op jit(solution)/shard_map/all_to_all | solution.py:53
  90.4 8.2 %all-to-all-done.1 = bf16[16,2,1440]{2,1,0:T(2,128)(2,1)S(1)} async-done(((bf16[16,2,1440]{2,1,0:T(2,128)(2,1)}), bf16[16,2,1440]{2,1,0:T(2,128)(2,1)S(1)}, u32[]{:S(2)}, u32[]{:S(2)}) %all-to-all-start.1) | async-done | bytes 92192 | tf_op jit(solution)/shard_map/all_to_all | solution.py:53
  101.2 5.0 multiply_reduce_fusion.1
  107.7 10.9 %all_to_all.138 = bf16[16,2,1440]{2,1,0:T(2,128)(2,1)S(1)} all-to-all(bf16[16,2,1440]{2,1,0:T(2,128)(2,1)S(1)} %reshape.166), channel_id=1, replica_groups=mesh['dp'=4,'gx'=4,'gy'=16] {'gy'}, dimensions={0} | all-to-all | bytes 184320 | tf_op jit(solution)/shard_map/all_to_all | solution.py:58
  122.3 9.6 %all_to_all.139 = bf16[4,2,15360]{2,1,0:T(2,128)(2,1)S(1)} all-to-all(bf16[4,2,15360]{2,1,0:T(2,128)(2,1)S(1)} %reshape.168), channel_id=1, replica_groups=mesh['dp'=4,'gx'=4,'gy'=16] {'gx'}, dimensions={0} | all-to-all | bytes 491520 | tf_op jit(solution)/shard_map/all_to_all | solution.py:60
  139.4 6.7 reshape.142
  146.1 11.0 %fusion.4 = bf16[1,16,2,20,2048]{4,3,2,1,0:T(8,128)(2,1)} fusion(f32[1,16,2,20,2048]{4,3,2,1,0:T(8,128)} %reshape.142, bf16[1,16,2,20,2048]{4,2,3,1,0:T(2,128)(2,1)} %param.5, bf16[16,2,20,2048]{3,1,2,0:T(2,128)(2,1)} %bitcast.208, bf16[20,20]{1,0:T(8,128)(2,1)S(1)} %copy-done), kind=kOutput, calls=%fused_computation.13 | convolution fusion | flops 81264640 | bytes 13108000 | tf_op jit(solution)/shard_map/bxyip,io->bxyop/dot_general | solution.py:70
  157.1 5.3 reshape.144
  168.0 3.8 reshape.161
  175.3 8.9 %all_to_all.140 = bf16[4,2,15360]{2,1,0:T(2,128)(2,1)} all-to-all(bf16[4,2,15360]{2,1,0:T(2,128)(2,1)S(1)} %reshape.170), channel_id=1, replica_groups=mesh['dp'=4,'gx'=4,'gy'=16] {'gx'}, dimensions={0} | all-to-all | bytes 491520 | tf_op jit(solution)/shard_map/all_to_all | solution.py:51
  184.1 6.0 reshape.171
  196.9 5.1 all-to-all-start.5
  204.3 6.3 all-to-all-done.5
  214.4 5.0 multiply_reduce_fusion
  225.2 4.9 fusion.31
  230.2 244.2 %psum.22 = f32[20,20]{0,1:T(8,128)S(1)} all-reduce(f32[20,20]{0,1:T(8,128)S(1)} %fusion.31), channel_id=1, replica_groups=mesh['dp'=4,'gx'=4,'gy'=16] {'gx','gy'}, use_global_device_ids=true, to_apply=%region_1.2 | all-reduce | flops 400 | bytes 3200 | tf_op jit(solution)/shard_map/psum | solution.py:76
  474.4 13.6 %psum.23 = f32[20,20]{0,1:T(8,128)S(1)} all-reduce(f32[20,20]{0,1:T(8,128)S(1)} %psum.22), channel_id=1, replica_groups=mesh['dp'=4,'gx'=4,'gy'=16] {'dp'}, use_global_device_ids=true, to_apply=%region_2.3 | all-reduce | flops 400 | bytes 3200 | tf_op jit(solution)/shard_map/psum | solution.py:77
  503.0 5.3 fusion.1
  515.8 7.2 %reshape.147 = f32[1,16,2,20,2048]{4,3,2,1,0:T(8,128)} reshape(f32[640,2048]{1,0:T(8,128)} %convolution_add_fusion) | data formatting | bytes 10485760 | tf_op jit(solution)/shard_map/reshape | solution.py:63
  523.1 4.5 fusion.12
  527.6 4.2 copy.189
  531.8 129.1 %all-reduce.2.cloned.1.call-done = bf16[24,24,20,20,3]{1,0,4,3,2:T(8,128)(2,1)} async-done(((bf16[24,24,20,20,3]{1,0,4,3,2:T(8,128)(2,1)}), bf16[24,24,20,20,3]{1,0,4,3,2:T(8,128)(2,1)}) %all-reduce.2.cloned.1.call-update) | async-done | bytes 1382416 | tf_op jit(solution)/shard_map/psum | solution.py:82
  660.9 10.2 %convert_element_type.284 = f32[24,24,20,20,3]{1,0,4,3,2:T(8,128)} convert(bf16[24,24,20,20,3]{1,0,4,3,2:T(8,128)(2,1)} %all-reduce.2.cloned.1.call-done) | non-fusion elementwise | flops 691200 | bytes 4147200 | tf_op jit(solution)/shard_map/convert_element_type | solution.py:82
  (91 shorter events, 78.3 us)
Async XLA Ops:
  7.2 139.0 %copy-start = (bf16[20,20]{1,0:T(8,128)(2,1)S(1)}, bf16[20,20]{1,0:T(8,128)(2,1)}, u32[]{:S(2)}) copy-start(bf16[20,20]{1,0:T(8,128)(2,1)} %param.7) | copy-start | bytes 2404
  60.0 10.3 %all-to-all-start = ((bf16[4,2,15360]{2,1,0:T(2,128)(2,1)}), bf16[4,2,15360]{2,1,0:T(2,128)(2,1)S(1)}, u32[]{:S(2)}, u32[]{:S(2)}) async-start(bf16[4,2,15360]{2,1,0:T(2,128)(2,1)} %reshape.162), calls=%async_computation | async-start | bytes 491520 | tf_op jit(solution)/shard_map/all_to_all | solution.py:51
  79.3 19.3 %all-to-all-start.1 = ((bf16[16,2,1440]{2,1,0:T(2,128)(2,1)}), bf16[16,2,1440]{2,1,0:T(2,128)(2,1)S(1)}, u32[]{:S(2)}, u32[]{:S(2)}) async-start(bf16[16,2,1440]{2,1,0:T(2,128)(2,1)} %reshape.164), calls=%async_computation.1 | async-start | bytes 196608 | tf_op jit(solution)/shard_map/all_to_all | solution.py:53
  119.1 16.2 %copy-start.1 = (bf16[2048,192]{0,1:T(8,128)(2,1)S(1)}, bf16[2048,192]{0,1:T(8,128)(2,1)}, u32[]{:S(2)}) copy-start(bf16[2048,192]{0,1:T(8,128)(2,1)} %convert_element_type.253) | copy-start | bytes 2359300
  196.9 13.7 %all-to-all-start.5 = ((bf16[16,2,1440]{2,1,0:T(2,128)(2,1)}), bf16[16,2,1440]{2,1,0:T(2,128)(2,1)S(1)}, u32[]{:S(2)}, u32[]{:S(2)}) async-start(bf16[16,2,1440]{2,1,0:T(2,128)(2,1)} %reshape.172), calls=%async_computation.5 | async-start | bytes 196608 | tf_op jit(solution)/shard_map/all_to_all | solution.py:53
  221.6 269.4 %all-to-all-start.6 = ((bf16[16,2,1440]{2,1,0:T(2,128)(2,1)}), bf16[16,2,1440]{2,1,0:T(2,128)(2,1)S(1)}, u32[]{:S(2)}, u32[]{:S(2)}) async-start(bf16[16,2,1440]{2,1,0:T(2,128)(2,1)} %reshape.174), calls=%async_computation.6 | async-start | bytes 196608 | tf_op jit(solution)/shard_map/all_to_all | solution.py:58
  230.2 272.8 %copy-start.3 = (f32[24,24,3,20]{1,0,2,3:T(8,128)S(1)}, f32[24,24,3,20]{1,0,2,3:T(8,128)}, u32[]{:S(2)}) copy-start(f32[24,24,3,20]{1,0,2,3:T(8,128)} %copy.187) | copy-start | bytes 414724
  499.5 8.8 %all-to-all-start.7 = ((bf16[4,2,15360]{2,1,0:T(2,128)(2,1)}), bf16[4,2,15360]{2,1,0:T(2,128)(2,1)S(1)}, u32[]{:S(2)}, u32[]{:S(2)}) async-start(bf16[4,2,15360]{2,1,0:T(2,128)(2,1)} %reshape.176), calls=%async_computation.7 | async-start | bytes 491520 | tf_op jit(solution)/shard_map/all_to_all | solution.py:60
  502.9 158.0 %all-reduce.2.cloned.1.call-start = ((), (), s32[]{:S(2)}) async-start(), calls=%async_computation.8 | async-start | bytes 14745600 | tf_op jit(solution)/shard_map/psum | solution.py:82
  515.8 7.2 %copy-start.2 = (bf16[1,16,2,20,2048]{4,3,2,1,0:T(8,128)(2,1)S(1)}, bf16[1,16,2,20,2048]{4,3,2,1,0:T(8,128)(2,1)}, u32[]{:S(2)}) copy-start(bf16[1,16,2,20,2048]{4,3,2,1,0:T(8,128)(2,1)} %fusion.4) | copy-start | bytes 7864324
Sparse Core Ops, SparseCore 0:
  508.5 152.4 all-reduce.1
